TPU v7x, 128 devices: a whole 4x4x4 slice. The times are simulated.
128 devices in a mesh: freq: 4 (over x), pts: 32 (over z, y, core).
Axes of the slice: x: 4, y: 4, z: 4, core: 2. Of those that a mesh axis runs over, the one named last changes fastest.
Arguments:
- snapshots: bfloat16 [131072, 4224], P(('freq', 'pts')), as said below
- weights: float32 [131072], P(('freq', 'pts')), may hold values from 0.25 to 4
- freq_bins: int32 [8], replicated, may hold values from 1 to 127
Outputs:
- spod_modes: float32 [2, 8, 32, 131072], P(None, None, None, ('freq', 'pts'))
- upper_factor: float32 [2, 8, 32, 32], P(None, 'freq')
Inputs may be any that keep to these rules, and one draw needn't show every extreme that they name: `snapshots`: fluctuations of pressure and velocity, with a few motions coherent over many points.
All inputs are finite; a program needn't handle non-finite values.
Results may differ from a plain program's by a relative error of at most 0.0045.
Values sent between devices are 32-bit elements; how exact they have to be, the bound alone decides.
A program may use at most 64 MiB of HBM per device.

v0:
```python
import math

import jax
import jax.numpy as jnp
from jax import lax
from jax.sharding import PartitionSpec as P

FREQ = 8
NB = 32
NFFT = 256


def dft_tables(freq_bins):
    moments = jnp.arange(NFFT, dtype=jnp.int32)
    phase_index = freq_bins[:, None] * moments[None, :] % NFFT
    angle = phase_index.astype(jnp.float32) * (2.0 * math.pi / NFFT)
    window = 0.5 - 0.5 * jnp.cos(moments.astype(jnp.float32) * (2.0 * math.pi / NFFT))
    table = jnp.concatenate(
        [window[None, :] * jnp.cos(angle), -window[None, :] * jnp.sin(angle)], axis=0
    )
    return table.astype(jnp.bfloat16)


def transform(snap_block, freq_bins):
    point_count = snap_block.shape[0]
    half_len = NFFT // 2
    dft_table = dft_tables(freq_bins)
    halves = snap_block.reshape(point_count, NB + 1, half_len)
    front_part = jnp.einsum(
        "ct,pbt->cbp", dft_table[:, :half_len], halves, preferred_element_type=jnp.float32
    )
    second = jnp.einsum(
        "ct,pbt->cbp", dft_table[:, half_len:], halves, preferred_element_type=jnp.float32
    )
    coefficients = front_part[:, :NB] + second[:, 1:]
    point_mean = jnp.sum(snap_block, axis=1, dtype=jnp.float32) / snap_block.shape[1]
    table_sum = jnp.sum(dft_table.astype(jnp.float32), axis=1)
    coefficients = (coefficients - table_sum[:, None, None] * point_mean[None, None, :]) * (
        1.0 / math.sqrt(NB * 0.375 * NFFT)
    )
    return coefficients.reshape(2, FREQ, NB, point_count)


def gram_matrix(part_real, part_imag):
    gram_real = jnp.einsum("fbp,fcp->fbc", part_real, part_real, precision=lax.Precision.HIGHEST)
    gram_real = gram_real + jnp.einsum(
        "fbp,fcp->fbc", part_imag, part_imag, precision=lax.Precision.HIGHEST
    )
    cross = jnp.einsum("fbp,fcp->fbc", part_real, part_imag, precision=lax.Precision.HIGHEST)
    return (gram_real, cross - jnp.swapaxes(cross, 1, 2))


def cholesky_upper(gram_real, gram_imag):
    order = gram_real.shape[-1]
    columns = jnp.arange(order)

    def cholesky_one_row(row_index, state_pair):
        upper_real, upper_imag = state_pair
        col_real = lax.dynamic_slice_in_dim(upper_real, row_index, 1, 2)
        col_imag = lax.dynamic_slice_in_dim(upper_imag, row_index, 1, 2)
        sum_real = jnp.sum(col_real * upper_real + col_imag * upper_imag, axis=1)
        sum_imag = jnp.sum(col_real * upper_imag - col_imag * upper_real, axis=1)
        rest_real = lax.dynamic_slice_in_dim(gram_real, row_index, 1, 1)[:, 0, :] - sum_real
        rest_imag = lax.dynamic_slice_in_dim(gram_imag, row_index, 1, 1)[:, 0, :] - sum_imag
        pivot = jnp.sqrt(lax.dynamic_slice_in_dim(rest_real, row_index, 1, 1))
        above_diag = columns[None, :] > row_index
        on_diag = columns[None, :] == row_index
        new_real = jnp.where(above_diag, rest_real / pivot, 0.0) + jnp.where(on_diag, pivot, 0.0)
        new_imag = jnp.where(above_diag, rest_imag / pivot, 0.0)
        upper_real = lax.dynamic_update_slice_in_dim(upper_real, new_real[:, None, :], row_index, 1)
        upper_imag = lax.dynamic_update_slice_in_dim(upper_imag, new_imag[:, None, :], row_index, 1)
        return (upper_real, upper_imag)

    zeros = jnp.zeros_like(gram_real)
    return lax.fori_loop(0, order, cholesky_one_row, (zeros, zeros))


def inverse_upper(upper_real, upper_imag):
    order = upper_real.shape[-1]
    columns = jnp.arange(order)
    identity = jnp.eye(order, dtype=upper_real.dtype)

    def inverse_one_row(step_index, state_pair):
        inv_real, inv_imag = state_pair
        row_index = order - 1 - step_index
        row_real = lax.dynamic_slice_in_dim(upper_real, row_index, 1, 1)[:, 0, :]
        row_imag = lax.dynamic_slice_in_dim(upper_imag, row_index, 1, 1)[:, 0, :]
        above_diag = columns[None, :] > row_index
        off_real = jnp.where(above_diag, row_real, 0.0)
        off_imag = jnp.where(above_diag, row_imag, 0.0)
        sum_real = jnp.sum(
            off_real[:, :, None] * inv_real - off_imag[:, :, None] * inv_imag, axis=1
        )
        sum_imag = jnp.sum(
            off_real[:, :, None] * inv_imag + off_imag[:, :, None] * inv_real, axis=1
        )
        pivot = lax.dynamic_slice_in_dim(row_real, row_index, 1, 1)
        unit_row = lax.dynamic_slice_in_dim(identity, row_index, 1, 0)
        new_real = (unit_row - sum_real) / pivot
        new_imag = -sum_imag / pivot
        inv_real = lax.dynamic_update_slice_in_dim(inv_real, new_real[:, None, :], row_index, 1)
        inv_imag = lax.dynamic_update_slice_in_dim(inv_imag, new_imag[:, None, :], row_index, 1)
        return (inv_real, inv_imag)

    zeros = jnp.zeros_like(upper_real)
    return lax.fori_loop(0, order, inverse_one_row, (zeros, zeros))


def recover(inv_real, inv_imag, part_real, part_imag, all_points):
    mode_real = jnp.einsum("fbc,fbp->fcp", inv_real, part_real, precision=lax.Precision.HIGHEST)
    mode_real = mode_real - jnp.einsum(
        "fbc,fbp->fcp", inv_imag, part_imag, precision=lax.Precision.HIGHEST
    )
    mode_imag = jnp.einsum("fbc,fbp->fcp", inv_imag, part_real, precision=lax.Precision.HIGHEST)
    mode_imag = mode_imag + jnp.einsum(
        "fbc,fbp->fcp", inv_real, part_imag, precision=lax.Precision.HIGHEST
    )
    return jnp.stack([mode_real, mode_imag]) * math.sqrt(all_points)


def body(snapshots, weights, freq_bins):
    point_count = snapshots.shape[0]
    all_points = lax.axis_size("freq") * lax.axis_size("pts") * point_count
    coefficients = transform(snapshots, freq_bins)
    scaled = coefficients * jnp.sqrt(weights / all_points)[None, None, None, :]
    gram_real, gram_imag = gram_matrix(scaled[0], scaled[1])
    gram_real, gram_imag = lax.psum((gram_real, gram_imag), ("freq", "pts"))
    upper_real, upper_imag = cholesky_upper(gram_real, gram_imag)
    inv_real, inv_imag = inverse_upper(upper_real, upper_imag)
    spod_modes = recover(inv_real, inv_imag, scaled[0], scaled[1], all_points)
    local_freqs = FREQ // lax.axis_size("freq")
    first_freq = lax.axis_index("freq") * local_freqs
    upper_real = lax.dynamic_slice_in_dim(upper_real, first_freq, local_freqs, 0)
    upper_imag = lax.dynamic_slice_in_dim(upper_imag, first_freq, local_freqs, 0)
    return (spod_modes, jnp.stack([upper_real, upper_imag]))


def solution(mesh):
    return jax.shard_map(
        body,
        mesh=mesh,
        in_specs=(P(("freq", "pts"), None), P(("freq", "pts")), P()),
        out_specs=(P(None, None, None, ("freq", "pts")), P(None, "freq", None, None)),
        check_vma=False,
    )
```

profile of v0, /device:TPU:1, one launch (start us, length us, event | category | flops | bytes accessed | tf_op | source)
XLA Modules:
  0.0 259.6 jit_solution(5524019808609106048)
XLA Ops:
  7.3 12.3 %copy.36 = bf16[1024,4224]{0,1:T(8,128)(2,1)} copy(bf16[1024,4224]{1,0:T(8,128)(2,1)} %param.7) | data formatting | bytes 17301504 | tf_op args[0]
  19.7 4.8 %convolution_bitcast_fusion = f32[16,33,1024]{2,0,1:T(8,128)S(1)} fusion(bf16[1024,33,128]{0,2,1:T(8,128)(2,1)} %bitcast.88, bf16[8,256]{1,0:T(8,128)(2,1)S(1)} %get-tuple-element.435, bf16[8,256]{1,0:T(8,128)(2,1)S(1)} %get-tuple-element.434), kind=kOutput, calls=%fused_computation.41 | convolution fusion | flops 138420224 | bytes 10821632 | tf_op jit(solution)/shard_map/ct,pbt->cbp/dot_general | solution.py:32
  24.6 1.1 copy-done
  25.6 1.2 convolution_bitcast_fusion.1
  27.0 2.1 copy-done.1
  29.1 1.2 convert_reduce_fusion
  30.9 1.2 copy_multiply_fusion
  32.1 1.1 fusion.22
  33.2 1.1 fusion.23
  35.0 1.7 convolution_add_fusion.1
  36.8 145.2 %all-reduce.3.cloned.1.call-done = (f32[8,32,32]{2,1,0:T(8,128)}, f32[8,32,32]{2,1,0:T(8,128)}) async-done(((f32[8,32,32]{2,1,0:T(8,128)}, f32[8,32,32]{2,1,0:T(8,128)}), (f32[8,32,32]{2,1,0:T(8,128)}, f32[8,32,32]{2,1,0:T(8,128)})) %all-reduce.3.cloned.1.call-update) | async-done | bytes 65552 | tf_op jit(solution)/shard_map/psum | solution.py:127
  182.1 41.2 %while.37 = (s32[]{:T(128)}, f32[8,32,32]{0,2,1:T(8,128)S(1)}, f32[8,32,32]{0,2,1:T(8,128)S(1)}, f32[8,32,32]{2,1,0:T(8,128)}, f32[8,32,32]{2,1,0:T(8,128)}, /*index=5*/s32[]{:T(128)}) while((s32[]{:T(128)}, f32[8,32,32]{0,2,1:T(8,128)S(1)}, f32[8,32,32]{0,2,1:T(8,128)S(1)}, f32[8,32,32]{2,1,0:T(8,128)}, ...), condition=%wide.region_7.8_spmd.clone.clone, body=%wide.region_4.7_spmd.clone.clone.sunk | while | flops 67146 | bytes 182009 | solution.py:75
  182.4 0.8 constant_dynamic-slice_fusion.11
  185.0 0.8 constant_dynamic-slice_fusion.11
  187.5 0.8 constant_dynamic-slice_fusion.11
  188.8 0.8 constant_dynamic-slice_fusion.11
  190.1 0.8 constant_dynamic-slice_fusion.11
  191.4 0.8 constant_dynamic-slice_fusion.11
  194.0 0.8 constant_dynamic-slice_fusion.11
  196.5 0.8 constant_dynamic-slice_fusion.11
  197.8 0.8 constant_dynamic-slice_fusion.11
  200.4 0.8 constant_dynamic-slice_fusion.11
  203.0 0.8 constant_dynamic-slice_fusion.11
  205.6 0.8 constant_dynamic-slice_fusion.11
  223.5 1.0 constant_dynamic-slice_fusion.8
  224.9 1.3 copy.51
  226.6 19.8 %while.36 = (s32[]{:T(128)}, f32[8,32,32]{2,1,0:T(8,128)S(1)}, f32[8,32,32]{2,1,0:T(8,128)S(1)}, f32[32,32]{1,0:T(8,128)S(1)}, f32[8,32,32]{2,0,1:T(8,128)S(1)},...) while((s32[]{:T(128)}, f32[8,32,32]{2,1,0:T(8,128)S(1)}, ...), condition=%wide.region_11.12_spmd.clone, body=%wide.region_8.11_spmd.clone.sunk | while | flops 66599 | bytes 84699 | solution.py:106
  246.3 1.0 fusion.21
  247.4 1.0 fusion.20
  248.4 1.1 fusion.19
  249.5 1.1 fusion.18
  251.2 1.5 maximum_multiply_fusion
  (559 shorter events, 51.4 us)
Async XLA Ops:
  7.2 174.9 %all-reduce.3.cloned.1.call-start = ((), (), s32[]{:S(2)}) async-start(), calls=%async_computation | async-start | bytes 524288 | tf_op jit(solution)/shard_map/psum | solution.py:127
  7.3 12.3 %copy-start.3 = (s32[8]{0:T(128)S(1)}, s32[8]{0:T(128)}, u32[]{:S(2)}) copy-start(s32[8]{0:T(128)} %param.9) | copy-start | bytes 100
  19.7 5.9 %copy-start = (bf16[1024,4224]{0,1:T(8,128)(2,1)S(1)}, bf16[1024,4224]{0,1:T(8,128)(2,1)}, u32[]{:S(2)}) copy-start(bf16[1024,4224]{0,1:T(8,128)(2,1)} %copy.36) | copy-start | bytes 25952260
  25.6 3.5 %copy-start.1 = (bf16[1024,4224]{1,0:T(8,128)(2,1)S(1)}, bf16[1024,4224]{1,0:T(8,128)(2,1)}, u32[]{:S(2)}) copy-start(bf16[1024,4224]{1,0:T(8,128)(2,1)} %param.7) | copy-start | bytes 25952260
  29.1 1.2 copy-start.2
Sparse Core Ops, SparseCore 0:
  36.9 145.0 all-reduce.2
where the time goes:
time: 262 us; the launch traced here: 260 us
  waiting for transfers between devices  145 us (55%)
  local copies, waits for them, and re-layouts  59.3 us (23%)
  other arithmetic  23.3 us (9%)
  matrix products  14.2 us (5%)
  between operations  14.2 us (5%)
  loops' own time  3.35 us (1%)
    psum x1, waiting for transfers between devices, body(): gram_real, gram_imag = lax.psum((gram_real, gram_imag), ('freq', 'pts'))  145 us
    dynamic_slice x64, local copies, waits for them, and re-layouts, cholesky_one_row(): lax.dynamic_slice_in_dim(gram_imag, row_index, 1, 1)[:, 0, :] - sum_imag  27.8 us
    unnamed x11, local copies, waits for them, and re-layouts  15.9 us
    dynamic_slice x32, local copies, waits for them, and re-layouts, inverse_one_row(): pivot = lax.dynamic_slice_in_dim(row_real, row_index, 1, 1)  5.96 us
    reduce_sum x32, other arithmetic, cholesky_one_row(): sum_imag = jnp.sum(col_real * upper_imag - col_imag * upper_real, axis=1)  5.96 us
  transfers between devices with their start and end apart: 1, of which 1 were waited for; matrix products, arithmetic and copies ran while one was open for 0% of the time, Pallas kernels for 0%

commit v1 on v0

v1 whole, which is shorter than its diff:
```python
import math

import jax
import jax.numpy as jnp
from jax import lax
from jax.experimental import pallas as pl
from jax.experimental.pallas import tpu as pltpu
from jax.sharding import PartitionSpec as P

FREQ = 8
NB = 32
NFFT = 256
HALF = NFFT // 2
SAMPLES = 4224
POINTS = 131072
LOCAL = 1024
CHUNK = 256
CHUNKS = LOCAL // CHUNK
GROUPS = 4
BAND = 9 * HALF
ROWS = 144
OWNERS = 8
SHARES = 16
MESH = pl.DeviceIdType.MESH
F32 = jnp.float32
BF16 = jnp.bfloat16
NT = (((1,), (1,)), ((), ()))


def place():
    x = lax.axis_index("freq")
    q = lax.axis_index("pts")
    core = lax.rem(q, 2)
    share = lax.div(q, 2)
    owner = x * 2 + core
    return owner, share


def device_of(owner, share):
    return (lax.div(owner, 2), share * 2 + lax.rem(owner, 2))


def owner_peer(owner, share, step):
    other = lax.rem(owner + step, OWNERS)
    return other, device_of(other, share)


def share_peer(owner, share, step):
    other = lax.rem(share + step, SHARES)
    return other, device_of(owner, other)


def build_band(bins_ref, band_ref, sums_ref):
    row = lax.broadcasted_iota(jnp.int32, (FREQ, NFFT), 0)
    moment = lax.broadcasted_iota(jnp.int32, (FREQ, NFFT), 1)
    bins = jnp.zeros((FREQ, NFFT), jnp.int32)
    for f in range(FREQ):
        bins = jnp.where(row == f, bins_ref[f], bins)
    angle = lax.bitwise_and(bins * moment, NFFT - 1).astype(F32) * (2.0 * math.pi / NFFT)
    window = 0.5 - 0.5 * jnp.cos(moment.astype(F32) * (2.0 * math.pi / NFFT))
    cosine = (window * jnp.cos(angle)).astype(BF16).astype(F32)
    sine = (-window * jnp.sin(angle)).astype(BF16).astype(F32)
    slot = lax.broadcasted_iota(jnp.int32, (8, HALF), 0)
    for q in range(9):
        tiles = []
        for c in range(2 * FREQ):
            table = cosine if c < FREQ else sine
            line = table[c % FREQ : c % FREQ + 1]
            front = jnp.broadcast_to(line[:, :HALF], (8, HALF))
            back = jnp.broadcast_to(line[:, HALF:], (8, HALF))
            tiles.append(jnp.where(slot == q, front, jnp.where(slot == q - 1, back, 0.0)))
        mark = 0 if q < 8 else 1
        tiles.append(jnp.where(slot == mark, 1.0, 0.0))
        tiles.append(jnp.zeros((8, HALF), F32))
        band_ref[:, q * HALF : (q + 1) * HALF] = jnp.concatenate(tiles, axis=0).astype(BF16)
    ones = jnp.ones((BAND, 128), BF16)
    sums_ref[...] = jnp.dot(band_ref[0:128, :], ones, preferred_element_type=F32)


def transform_chunk(chunk, weights_ref, x_ref, band_ref, sums_ref, parts_ref):
    band = band_ref[...]
    groups = []
    total = jnp.zeros((1, CHUNK), F32)
    for g in range(GROUPS):
        x = x_ref[chunk, :, g * 8 * HALF : g * 8 * HALF + BAND]
        d = lax.dot_general(band, x, NT, preferred_element_type=F32)
        groups.append(d)
        total = total + d[128:129]
        if g == GROUPS - 1:
            total = total + d[129:130]
    mean = total * (1.0 / SAMPLES)
    w = jnp.concatenate([weights_ref[2 * chunk : 2 * chunk + 1], weights_ref[2 * chunk + 1 : 2 * chunk + 2]], axis=1)
    scale = jnp.sqrt(w * (1.0 / POINTS)) * (1.0 / math.sqrt(NB * 0.375 * NFFT))
    cols = slice(chunk * CHUNK, (chunk + 1) * CHUNK)
    for f in range(FREQ):
        for part in range(2):
            c = part * FREQ + f
            sums = sums_ref[c * 8 : c * 8 + 8, :]
            away = jnp.concatenate([sums, sums], axis=1) * mean
            y = jnp.concatenate([(d[c * 8 : c * 8 + 8] - away) * scale for d in groups], axis=0)
            hi = y.astype(BF16)
            lo = (y - hi.astype(F32)).astype(BF16)
            parts_ref[f, part * NB : (part + 1) * NB, cols] = hi
            parts_ref[f, 64 + part * NB : 64 + (part + 1) * NB, cols] = lo
            parts_ref[f, 128 + part * NB : 128 + (part + 1) * NB, cols] = hi


def packed_gram(parts_ref, f):
    hi = parts_ref[f, 0:64, :]
    lo = parts_ref[f, 64:128, :]
    s = lax.dot_general(hi, hi, NT, preferred_element_type=F32)
    s = s + lax.dot_general(hi, lo, NT, preferred_element_type=F32)
    s = s + lax.dot_general(lo, hi, NT, preferred_element_type=F32)
    gram_real = s[0:32, 0:32] + s[32:64, 32:64]
    gram_imag = s[0:32, 32:64] - s[32:64, 0:32]
    i = lax.broadcasted_iota(jnp.int32, (NB, NB), 0)
    j = lax.broadcasted_iota(jnp.int32, (NB, NB), 1)
    packed = jnp.where(i >= j, gram_real, gram_imag)
    return jnp.concatenate([packed[8 * r : 8 * r + 8] for r in range(4)], axis=1)


def eliminate(packed):
    p = jnp.concatenate([packed[:, 32 * r : 32 * r + 32] for r in range(4)], axis=0)
    t = p.T
    i = lax.broadcasted_iota(jnp.int32, (NB, NB), 0)
    j = lax.broadcasted_iota(jnp.int32, (NB, NB), 1)
    real = jnp.where(i >= j, p, t)
    imag = jnp.where(i < j, p, jnp.where(i > j, -t, 0.0))
    eye = jnp.where(i == j, 1.0, 0.0)
    zero = jnp.zeros((NB, NB), F32)
    whole = jnp.concatenate([real, imag, eye, zero], axis=1)
    turned = jnp.concatenate([-imag, real, zero, eye], axis=1)
    a = [whole[8 * u : 8 * u + 8] for u in range(4)]
    b = [turned[8 * u : 8 * u + 8] for u in range(4)]
    pivots = [jnp.ones((8, 128), F32) for u in range(4)]
    sub = lax.broadcasted_iota(jnp.int32, (8, 128), 0)
    for k in range(NB):
        v, s = k // 8, k % 8
        col_real = {u: jnp.broadcast_to(a[u][:, k : k + 1], (8, 128)) for u in range(v, 4)}
        col_imag = {u: jnp.broadcast_to(a[u][:, 32 + k : 33 + k], (8, 128)) for u in range(v, 4)}
        pivot = jnp.broadcast_to(col_real[v][s : s + 1], (8, 128))
        over = 1.0 / pivot
        row = jnp.broadcast_to(a[v][s : s + 1], (8, 128)) * over
        row_turned = jnp.broadcast_to(b[v][s : s + 1], (8, 128)) * over
        pivots[v] = jnp.where(sub == s, pivot, pivots[v])
        for u in range(v, 4):
            m_real, m_imag = col_real[u], col_imag[u]
            if u == v:
                m_real = jnp.where(sub > s, m_real, 0.0)
                m_imag = jnp.where(sub > s, m_imag, 0.0)
            a[u], b[u] = (
                a[u] - (m_real * row + m_imag * row_turned),
                b[u] - (m_real * row_turned - m_imag * row),
            )
    return [a[u] * (1.0 / jnp.sqrt(pivots[u])) for u in range(4)]


def wait_bytes(ref, sem):
    pltpu.make_async_copy(ref, ref, sem).wait()


def kernel(
    bins_ref, weights_ref, snap_ref, modes_ref, upper_ref,
    x_ref, band_ref, sums_ref, parts_ref, out_ref, pack_ref, got_a, got_b, got_c, got_r,
    in_sem, out_sem, send_a, recv_a, send_b, recv_b, send_c, recv_c, send_r, recv_r,
):
    owner, share = place()
    core = lax.rem(owner, 2)
    loads = []
    for chunk in range(CHUNKS):
        load = pltpu.make_async_copy(snap_ref.at[chunk * CHUNK : (chunk + 1) * CHUNK, :], x_ref.at[chunk], in_sem.at[chunk])
        load.start()
        loads.append(load)
    barrier = pltpu.get_barrier_semaphore()
    for step in range(1, OWNERS):
        pl.semaphore_signal(barrier, inc=1, device_id=owner_peer(owner, share, step)[1], device_id_type=MESH)
    for step in range(1, SHARES):
        pl.semaphore_signal(barrier, inc=1, device_id=share_peer(owner, share, step)[1], device_id_type=MESH)

    build_band(bins_ref, band_ref, sums_ref)
    for chunk in range(CHUNKS):
        loads[chunk].wait()
        transform_chunk(chunk, weights_ref, x_ref, band_ref, sums_ref, parts_ref)
    for f in range(FREQ):
        pack_ref[f] = packed_gram(parts_ref, f)

    pl.semaphore_wait(barrier, OWNERS - 1 + SHARES - 1)
    for step in range(1, OWNERS):
        other, device = owner_peer(owner, share, step)
        pltpu.make_async_remote_copy(
            src_ref=pack_ref.at[other], dst_ref=got_a.at[owner], send_sem=send_a, recv_sem=recv_a,
            device_id=device, device_id_type=MESH,
        ).start()
    got_a[owner] = pack_ref[owner]
    wait_bytes(got_a.at[0 : OWNERS - 1], recv_a)
    part = got_a[0]
    for n in range(1, OWNERS):
        part = part + got_a[n]

    got_b[share] = part
    for step in range(1, SHARES):
        other, device = share_peer(owner, share, step)
        pltpu.make_async_remote_copy(
            src_ref=got_b.at[share], dst_ref=got_b.at[share], send_sem=send_b, recv_sem=recv_b,
            device_id=device, device_id_type=MESH,
        ).start()
    wait_bytes(got_b.at[0 : SHARES - 1], recv_b)
    packed = got_b[0]
    for n in range(1, SHARES):
        packed = packed + got_b[n]

    rows = eliminate(packed)
    lane = lax.broadcasted_iota(jnp.int32, (8, 128), 1)
    for h in range(2):
        even, odd = rows[2 * h], rows[2 * h + 1]
        odd_far = pltpu.roll(odd, 64, 1)
        got_c[owner, h] = jnp.where(lane < 64, odd_far, even)
        got_r[core, h] = jnp.where(lane < 64, even, odd_far)
    for step in range(1, OWNERS):
        other, device = owner_peer(owner, share, step)
        pltpu.make_async_remote_copy(
            src_ref=got_c.at[owner], dst_ref=got_c.at[owner], send_sem=send_c, recv_sem=recv_c,
            device_id=device, device_id_type=MESH,
        ).start()
    x = lax.div(owner, 2)
    pltpu.make_async_remote_copy(
        src_ref=got_r.at[core], dst_ref=got_r.at[core], send_sem=send_r, recv_sem=recv_r,
        device_id=(x, share * 2 + 1 - core), device_id_type=MESH,
    ).start()
    wait_bytes(got_c.at[0 : OWNERS - 1], recv_c)

    stores = []
    for f in range(FREQ):
        inv = jnp.concatenate(
            [got_c[f, 0][:, 64:], got_c[f, 0][:, :64], got_c[f, 1][:, 64:], got_c[f, 1][:, :64]], axis=0
        ) * math.sqrt(POINTS)
        inv = jnp.concatenate([inv, jnp.concatenate([-inv[:, 32:], inv[:, :32]], axis=1)], axis=0)
        hi = inv.astype(BF16)
        lo = (inv - hi.astype(F32)).astype(BF16)
        left = jnp.concatenate([hi, hi, lo], axis=1)
        modes = jnp.dot(left, parts_ref[f], preferred_element_type=F32)
        out_ref[0, f] = modes[0:32]
        out_ref[1, f] = modes[32:64]
        store = pltpu.make_async_copy(out_ref.at[:, f], modes_ref.at[:, f], out_sem.at[f])
        store.start()
        stores.append(store)

    wait_bytes(got_r.at[0], recv_r)
    i = lax.broadcasted_iota(jnp.int32, (NB, NB), 0)
    j = lax.broadcasted_iota(jnp.int32, (NB, NB), 1)
    for n in range(2):
        both = jnp.concatenate(
            [got_r[n, 0][:, :64], got_r[n, 0][:, 64:], got_r[n, 1][:, :64], got_r[n, 1][:, 64:]], axis=0
        )
        upper_ref[0, n] = jnp.where(j >= i, both[:, :32], 0.0)
        upper_ref[1, n] = jnp.where(j > i, both[:, 32:], 0.0)
    wait_bytes(got_a.at[0 : OWNERS - 1], send_a)
    wait_bytes(got_b.at[0 : SHARES - 1], send_b)
    wait_bytes(got_c.at[0 : OWNERS - 1], send_c)
    wait_bytes(got_r.at[0], send_r)
    for store in stores:
        store.wait()


def body(snapshots, weights, freq_bins):
    dma = pltpu.SemaphoreType.DMA
    return pl.pallas_call(
        kernel,
        out_shape=(
            jax.ShapeDtypeStruct((2, FREQ, NB, LOCAL), F32),
            jax.ShapeDtypeStruct((2, 2, NB, NB), F32),
        ),
        in_specs=[
            pl.BlockSpec(memory_space=pltpu.SMEM),
            pl.BlockSpec(memory_space=pltpu.VMEM),
            pl.BlockSpec(memory_space=pltpu.HBM),
        ],
        out_specs=(pl.BlockSpec(memory_space=pltpu.HBM), pl.BlockSpec(memory_space=pltpu.VMEM)),
        scratch_shapes=[
            pltpu.VMEM((CHUNKS, CHUNK, SAMPLES), BF16),
            pltpu.VMEM((ROWS, BAND), BF16),
            pltpu.VMEM((128, 128), F32),
            pltpu.VMEM((FREQ, 192, LOCAL), BF16),
            pltpu.VMEM((2, FREQ, NB, LOCAL), F32),
            pltpu.VMEM((FREQ, 8, 128), F32),
            pltpu.VMEM((OWNERS, 8, 128), F32),
            pltpu.VMEM((SHARES, 8, 128), F32),
            pltpu.VMEM((OWNERS, 2, 8, 128), F32),
            pltpu.VMEM((2, 2, 8, 128), F32),
            dma((CHUNKS,)), dma((FREQ,)),
            dma, dma, dma, dma, dma, dma, dma, dma,
        ],
        compiler_params=pltpu.CompilerParams(
            collective_id=0, has_side_effects=True, vmem_limit_bytes=60 * 1024 * 1024
        ),
        cost_estimate=pl.CostEstimate(flops=2_000_000_000, bytes_accessed=11_000_000, transcendentals=0),
    )(freq_bins, weights.reshape(8, 128), snapshots)


def solution(mesh):
    return jax.shard_map(
        body,
        mesh=mesh,
        in_specs=(P(("freq", "pts"), None), P(("freq", "pts")), P()),
        out_specs=(P(None, None, None, ("freq", "pts")), P(None, "freq", None, None)),
        check_vma=False,
    )
```

time: 262 us -> 36.1 us (0.14)
  waiting for transfers between devices: 145 us -> 0 us
  local copies, waits for them, and re-layouts: 59.3 us -> 3.82 us
  Pallas kernels: 0 us -> 31.5 us
  other arithmetic: 23.3 us -> 0 us
  matrix products: 14.2 us -> 0 us
  between operations: 14.2 us -> 0.65 us
  loops' own time: 3.35 us -> 0 us
    psum x1 -> x0, waiting for transfers between devices: 145 us -> none  [body(): gram_real, gram_imag = lax.psum((gram_real, gram_imag), ('freq', 'pts'))]
    dynamic_slice x196 -> x0, local copies, waits for them, and re-layouts: 40.5 us -> none  [the longest x64 27.8 us: cholesky_one_row(): lax.dynamic_slice_in_dim(gram_imag, row_index, 1, 1)[:, 0, :] - sum_imag]
    pallas_call x0 -> x1, Pallas kernels: none -> 31.5 us  [body(): pl.pallas_call(kernel, out_shape=(jax.ShapeDtypeStruct((2, FREQ, NB, LOCA...]
    dot_general x9 -> x0, matrix products: 14.2 us -> none  [the longest x1 4.84 us: transform(): jnp.einsum('ct,pbt->cbp', dft_table[:, half_len:], halves, preferred_elem...]
    reduce_sum x66 -> x0, other arithmetic: 12.1 us -> none  [the longest x32 5.96 us: cholesky_one_row(): sum_imag = jnp.sum(col_real * upper_imag - col_imag * upper_real, axis=1)]
    unnamed x11 -> x4, local copies, waits for them, and re-layouts: 15.9 us -> 3.82 us
    another operation x2 -> x0, loops' own time: 3.35 us -> none  [the longest x1 2.76 us: inverse_upper(): return lax.fori_loop(0, order, inverse_one_row, (zeros, zeros))]
    mul x3 -> x0, other arithmetic: 2.83 us -> none  [the longest x1 1.53 us: recover(): return jnp.stack([mode_real, mode_imag]) * math.sqrt(all_points)]
  transfers between devices with their start and end apart: 1 -> 0, of which waited for: 1 -> 0; matrix products, arithmetic and copies ran while one was open for 0% -> 0% of each run, Pallas kernels for 0% -> 0%
where the time goes in v1:
time: 36.1 us; the launch traced here: 36 us
  Pallas kernels  31.5 us (87%)
  local copies, waits for them, and re-layouts  3.82 us (11%)
  between operations  0.65 us (2%)
    pallas_call x1, Pallas kernels, body(): pl.pallas_call(kernel, out_shape=(jax.ShapeDtypeStruct((2, FREQ, NB, LOCA...  31.5 us
    unnamed x4, local copies, waits for them, and re-layouts  3.82 us

profile of v1, /device:TPU:1, one launch (start us, length us, event | category | flops | bytes accessed | tf_op | source)
XLA Modules:
  0.0 36.0 jit_solution(13381919449858582601)
XLA Ops:
  0.6 31.5 %shard_map.50 = (f32[2,8,32,1024]{3,2,1,0:T(8,128)}, f32[2,2,32,32]{3,2,1,0:T(8,128)}) custom-call(s32[8]{0:T(128)} %bins_ref.1, f32[8,128]{1,0:T(8,128)} %bitcast.1, bf16[1024,4224]{1,0:T(8,128)(2,1)} %snap_ref.1), custom_call_target="tpu_custom_call" | custom-call | flops 2000000000 | bytes 11000000 | tf_op jit(solution)/shard_map/pallas_call | solution.py:267
  32.1 0.0 copy-start
  32.2 3.2 %copy.7 = f32[2,8,32,1024]{3,2,1,0:T(8,128)} copy(f32[2,8,32,1024]{3,2,1,0:T(8,128)} %get-tuple-element.4) | data formatting | bytes 4194304
  35.3 0.0 copy-done
  35.3 0.6 %copy.8 = f32[2,2,32,32]{3,2,1,0:T(8,128)} copy(f32[2,2,32,32]{3,2,1,0:T(8,128)S(1)} %copy-done) | data formatting | bytes 32768
Async XLA Ops:
  32.1 3.2 %copy-start = (f32[2,2,32,32]{3,2,1,0:T(8,128)S(1)}, f32[2,2,32,32]{3,2,1,0:T(8,128)}, u32[]{:S(2)}) copy-start(f32[2,2,32,32]{3,2,1,0:T(8,128)} %get-tuple-element.5) | copy-start | bytes 49156

commit v2 on v1

v2 whole, which is shorter than its diff:
```python
import math

import jax
import jax.numpy as jnp
from jax import lax
from jax.experimental import pallas as pl
from jax.experimental.pallas import tpu as pltpu
from jax.sharding import PartitionSpec as P

FREQ = 8
NB = 32
NFFT = 256
HALF = NFFT // 2
SAMPLES = 4224
POINTS = 131072
LOCAL = 1024
CHUNK = 256
CHUNKS = LOCAL // CHUNK
GROUPS = 4
BAND = 9 * HALF
ROWS = 144
ROW = 4
SHARES = 16
WIDTH = 4
GRAM_MIB = 44
MODES_MIB = 40
ROW_STEPS = (2, 1, 3)
PLANE_STEPS = (10, 6, 9, 11, 14, 2, 5, 7, 8, 13, 15, 1, 3, 4, 12)
MESH = pl.DeviceIdType.MESH
F32 = jnp.float32
BF16 = jnp.bfloat16
NT = (((1,), (1,)), ((), ()))


def place():
    x = lax.axis_index("freq")
    q = lax.axis_index("pts")
    return x, lax.div(q, 2), lax.rem(q, 2)


def row_peer(x, share, core, step):
    other = lax.rem(x + step, ROW)
    return other, (other, share * 2 + core)


def plane_peer(x, share, core, step):
    z, y = lax.div(share, 4), lax.rem(share, 4)
    other = lax.rem(z + step // 4, 4) * 4 + lax.rem(y + step % 4, 4)
    return other, (x, other * 2 + core)


def build_band(bins_ref, band_ref, sums_ref):
    row = lax.broadcasted_iota(jnp.int32, (FREQ, NFFT), 0)
    moment = lax.broadcasted_iota(jnp.int32, (FREQ, NFFT), 1)
    bins = jnp.zeros((FREQ, NFFT), jnp.int32)
    for f in range(FREQ):
        bins = jnp.where(row == f, bins_ref[f], bins)
    angle = lax.bitwise_and(bins * moment, NFFT - 1).astype(F32) * (2.0 * math.pi / NFFT)
    window = 0.5 - 0.5 * jnp.cos(moment.astype(F32) * (2.0 * math.pi / NFFT))
    cosine = (window * jnp.cos(angle)).astype(BF16).astype(F32)
    sine = (-window * jnp.sin(angle)).astype(BF16).astype(F32)
    slot = lax.broadcasted_iota(jnp.int32, (8, HALF), 0)
    for q in range(9):
        tiles = []
        for c in range(2 * FREQ):
            table = cosine if c < FREQ else sine
            line = table[c % FREQ : c % FREQ + 1]
            front = jnp.broadcast_to(line[:, :HALF], (8, HALF))
            back = jnp.broadcast_to(line[:, HALF:], (8, HALF))
            tiles.append(jnp.where(slot == q, front, jnp.where(slot == q - 1, back, 0.0)))
        mark = 0 if q < 8 else 1
        tiles.append(jnp.where(slot == mark, 1.0, 0.0))
        tiles.append(jnp.zeros((8, HALF), F32))
        band_ref[:, q * HALF : (q + 1) * HALF] = jnp.concatenate(tiles, axis=0).astype(BF16)
    ones = jnp.ones((BAND, 128), BF16)
    sums_ref[...] = jnp.dot(band_ref[0:128, :], ones, preferred_element_type=F32)


def transform_chunk(chunk, weights_ref, x_ref, band_ref, sums_ref, parts_ref):
    band = band_ref[...]
    groups = []
    total = jnp.zeros((1, CHUNK), F32)
    for g in range(GROUPS):
        x = x_ref[chunk, :, g * 8 * HALF : g * 8 * HALF + BAND]
        d = lax.dot_general(band, x, NT, preferred_element_type=F32)
        groups.append(d)
        total = total + d[128:129]
        if g == GROUPS - 1:
            total = total + d[129:130]
    mean = total * (1.0 / SAMPLES)
    w = jnp.concatenate([weights_ref[2 * chunk : 2 * chunk + 1], weights_ref[2 * chunk + 1 : 2 * chunk + 2]], axis=1)
    scale = jnp.sqrt(w * (1.0 / POINTS)) * (1.0 / math.sqrt(NB * 0.375 * NFFT))
    cols = slice(chunk * CHUNK, (chunk + 1) * CHUNK)
    for f in range(FREQ):
        for part in range(2):
            c = part * FREQ + f
            sums = sums_ref[c * 8 : c * 8 + 8, :]
            away = jnp.concatenate([sums, sums], axis=1) * mean
            y = jnp.concatenate([(d[c * 8 : c * 8 + 8] - away) * scale for d in groups], axis=0)
            hi = y.astype(BF16)
            lo = (y - hi.astype(F32)).astype(BF16)
            parts_ref[f, part * NB : (part + 1) * NB, cols] = hi
            parts_ref[f, 64 + part * NB : 64 + (part + 1) * NB, cols] = lo
            parts_ref[f, 128 + part * NB : 128 + (part + 1) * NB, cols] = hi


def add_gram(parts_ref, gram_ref, chunk):
    cols = slice(chunk * CHUNK, (chunk + 1) * CHUNK)
    for f in range(FREQ):
        hi = parts_ref[f, 0:64, cols]
        lo = parts_ref[f, 64:128, cols]
        s = lax.dot_general(hi, hi, NT, preferred_element_type=F32)
        s = s + lax.dot_general(hi, lo, NT, preferred_element_type=F32)
        s = s + lax.dot_general(lo, hi, NT, preferred_element_type=F32)
        gram_ref[f] = s if chunk == 0 else gram_ref[f] + s


def packed_gram(gram_ref, f):
    s = gram_ref[f]
    gram_real = s[0:32, 0:32] + s[32:64, 32:64]
    gram_imag = s[0:32, 32:64] - s[32:64, 0:32]
    i = lax.broadcasted_iota(jnp.int32, (NB, NB), 0)
    j = lax.broadcasted_iota(jnp.int32, (NB, NB), 1)
    packed = jnp.where(i >= j, gram_real, gram_imag)
    return jnp.concatenate([packed[8 * r : 8 * r + 8] for r in range(4)], axis=1)


def lanes(tile, k):
    return jnp.broadcast_to(tile[:, k : k + 1], (8, 128))


def sublanes(tile, s):
    return jnp.broadcast_to(tile[s : s + 1], (8, 128))


def unpack_gram(packed):
    p = jnp.concatenate([packed[:, 32 * r : 32 * r + 32] for r in range(4)], axis=0)
    t = p.T
    i = lax.broadcasted_iota(jnp.int32, (NB, NB), 0)
    j = lax.broadcasted_iota(jnp.int32, (NB, NB), 1)
    real = jnp.where(i >= j, p, t)
    imag = jnp.where(i < j, p, jnp.where(i > j, -t, 0.0))
    eye = jnp.where(i == j, 1.0, 0.0)
    zero = jnp.zeros((NB, NB), F32)
    whole = jnp.concatenate([real, imag, eye, zero], axis=1)
    turned = jnp.concatenate([-imag, real, zero, eye], axis=1)
    return [whole[8 * u : 8 * u + 8] for u in range(4)], [turned[8 * u : 8 * u + 8] for u in range(4)]


def eliminate(packed):
    a, b = unpack_gram(packed)
    pivots = [jnp.ones((8, 128), F32) for _ in range(4)]
    sub = lax.broadcasted_iota(jnp.int32, (8, 128), 0)
    for first in range(0, NB, WIDTH):
        v, s = first // 8, first % 8
        last = s + WIDTH == 8
        col_real = {u: [lanes(a[u], first + j) for j in range(WIDTH)] for u in range(v, 4)}
        col_imag = {u: [lanes(a[u], NB + first + j) for j in range(WIDTH)] for u in range(v, 4)}
        rows = [sublanes(a[v], s + j) for j in range(WIDTH)]
        turned = [sublanes(b[v], s + j) for j in range(WIDTH)]
        block_real = [[sublanes(col_real[v][l], s + i) for l in range(i + 1)] for i in range(WIDTH)]
        block_imag = [[sublanes(col_imag[v][l], s + i) for l in range(i)] for i in range(WIDTH)]
        over = []
        for j in range(WIDTH):
            pivot = block_real[j][j]
            inverse = 1.0 / pivot
            over.append(inverse)
            pivots[v] = jnp.where(sub == s + j, pivot, pivots[v])
            below = range(j + 1, WIDTH)
            m_real = {i: block_real[i][j] * inverse for i in below}
            m_imag = {i: block_imag[i][j] * inverse for i in below}
            for i in below:
                for l in range(j + 1, i + 1):
                    other_real, other_imag = block_real[l][j], block_imag[l][j]
                    block_real[i][l] = block_real[i][l] - (m_real[i] * other_real + m_imag[i] * other_imag)
                    if l < i:
                        block_imag[i][l] = block_imag[i][l] - (m_imag[i] * other_real - m_real[i] * other_imag)
            for i in below:
                rows[i], turned[i] = (
                    rows[i] - (m_real[i] * rows[j] + m_imag[i] * turned[j]),
                    turned[i] - (m_real[i] * turned[j] - m_imag[i] * rows[j]),
                )
            for u in range(v + 1 if last else v, 4):
                x, y = col_real[u][j], col_imag[u][j]
                for l in below:
                    col_real[u][l] = col_real[u][l] - (x * m_real[l] + y * m_imag[l])
                    col_imag[u][l] = col_imag[u][l] - (y * m_real[l] - x * m_imag[l])
        for u in range(v, 4):
            new_a, new_b = a[u], b[u]
            if u > v or not last:
                for j in range(WIDTH):
                    x, y = col_real[u][j], col_imag[u][j]
                    row, row_turned = rows[j] * over[j], turned[j] * over[j]
                    new_a = new_a - (x * row + y * row_turned)
                    new_b = new_b - (x * row_turned - y * row)
                if u == v and s > 0:
                    new_a = jnp.where(sub < s, a[u], new_a)
                    new_b = jnp.where(sub < s, b[u], new_b)
            if u == v:
                for j in range(WIDTH):
                    new_a = jnp.where(sub == s + j, rows[j], new_a)
                    new_b = jnp.where(sub == s + j, turned[j], new_b)
            a[u], b[u] = new_a, new_b
    return [a[u] * (1.0 / jnp.sqrt(pivots[u])) for u in range(4)]


def wait_bytes(ref, sem):
    pltpu.make_async_copy(ref, ref, sem).wait()


def gram_kernel(
    bins_ref, weights_ref, snap_ref, parts_ref, lower_ref, upper_ref,
    bins_here, weights_here, x_ref, band_ref, sums_ref, gram_ref, pack_ref, got_s, half_ref, got_x, got_p,
    small_sem, in_sem, s_sems, x_sems, p_sems, l_sems, c_sems, r_sems,
):
    x, share, core = place()
    sibling = (x, share * 2 + 1 - core)
    smalls = [
        pltpu.make_async_copy(bins_ref, bins_here, small_sem.at[0]),
        pltpu.make_async_copy(weights_ref, weights_here, small_sem.at[1]),
    ]
    for small in smalls:
        small.start()
    loads = []
    for chunk in range(CHUNKS):
        load = pltpu.make_async_copy(snap_ref.at[chunk * CHUNK : (chunk + 1) * CHUNK, :], x_ref.at[chunk], in_sem.at[chunk])
        load.start()
        loads.append(load)

    def send(src, dst, sems, device):
        pltpu.make_async_remote_copy(
            src_ref=src, dst_ref=dst, send_sem=sems.at[0], recv_sem=sems.at[1], device_id=device, device_id_type=MESH
        ).start()

    barrier = pltpu.get_barrier_semaphore()
    pl.semaphore_signal(barrier, inc=1, device_id=sibling, device_id_type=MESH)
    for step in ROW_STEPS:
        pl.semaphore_signal(barrier, inc=1, device_id=row_peer(x, share, core, step)[1], device_id_type=MESH)
    for step in PLANE_STEPS:
        pl.semaphore_signal(barrier, inc=1, device_id=plane_peer(x, share, core, step)[1], device_id_type=MESH)

    for small in smalls:
        small.wait()
    build_band(bins_here, band_ref, sums_ref)
    for chunk in range(CHUNKS):
        loads[chunk].wait()
        transform_chunk(chunk, weights_here, x_ref, band_ref, sums_ref, parts_ref)
        add_gram(parts_ref, gram_ref, chunk)
    for f in range(FREQ):
        pack_ref[f % 2, f // 2] = packed_gram(gram_ref, f)
    pl.semaphore_wait(barrier, 1 + ROW - 1 + SHARES - 1)

    send(pack_ref.at[1 - core], got_s, s_sems, sibling)
    wait_bytes(got_s, s_sems.at[1])
    half_ref[...] = pack_ref[core] + got_s[...]

    for step in ROW_STEPS:
        other, device = row_peer(x, share, core, step)
        send(half_ref.at[other], got_x.at[x], x_sems, device)
    got_x[x] = half_ref[x]
    wait_bytes(got_x.at[0 : ROW - 1], x_sems.at[1])
    got_p[share] = (got_x[0] + got_x[1]) + (got_x[2] + got_x[3])

    for step in PLANE_STEPS:
        other, device = plane_peer(x, share, core, step)
        send(got_p.at[share], got_p.at[share], p_sems, device)
    wait_bytes(got_p.at[0 : SHARES - 1], p_sems.at[1])
    terms = [got_p[n] for n in range(SHARES)]
    while len(terms) > 1:
        terms = [terms[n] + terms[n + 1] for n in range(0, len(terms), 2)]

    rows = eliminate(terms[0])
    lane = lax.broadcasted_iota(jnp.int32, (8, 128), 1)
    for h in range(2):
        even, odd = rows[2 * h], rows[2 * h + 1]
        odd_far = pltpu.roll(odd, 64, 1)
        lower_ref[core, x, h] = jnp.where(lane < 64, odd_far, even)
        upper_ref[core, h] = jnp.where(lane < 64, even, odd_far)
    mine = lower_ref.at[core, x]
    for step in ROW_STEPS:
        other, device = row_peer(x, share, core, step)
        send(mine, mine, l_sems, device)
    send(upper_ref.at[core], upper_ref.at[core], r_sems, sibling)
    wait_bytes(lower_ref.at[0, 0 : ROW - 1], l_sems.at[1])
    send(lower_ref.at[core], lower_ref.at[core], c_sems, sibling)
    wait_bytes(lower_ref.at[0], c_sems.at[1])
    wait_bytes(upper_ref.at[0], r_sems.at[1])

    wait_bytes(got_s, s_sems.at[0])
    wait_bytes(got_x.at[0 : ROW - 1], x_sems.at[0])
    wait_bytes(got_p.at[0 : SHARES - 1], p_sems.at[0])
    wait_bytes(lower_ref.at[0, 0 : ROW - 1], l_sems.at[0])
    wait_bytes(lower_ref.at[0], c_sems.at[0])
    wait_bytes(upper_ref.at[0], r_sems.at[0])


def modes_kernel(parts_ref, lower_ref, packed_ref, modes_ref, upper_ref, out_ref, up_ref, out_sem, up_sem):
    i = lax.broadcasted_iota(jnp.int32, (NB, NB), 0)
    j = lax.broadcasted_iota(jnp.int32, (NB, NB), 1)
    for n in range(2):
        both = jnp.concatenate(
            [packed_ref[n, 0][:, :64], packed_ref[n, 0][:, 64:], packed_ref[n, 1][:, :64], packed_ref[n, 1][:, 64:]], axis=0
        )
        up_ref[0, n] = jnp.where(j >= i, both[:, :32], 0.0)
        up_ref[1, n] = jnp.where(j > i, both[:, 32:], 0.0)
    up_store = pltpu.make_async_copy(up_ref, upper_ref, up_sem)
    up_store.start()
    stores = []
    for f in range(FREQ):
        low, high = lower_ref[f % 2, f // 2, 0], lower_ref[f % 2, f // 2, 1]
        inv = jnp.concatenate([low[:, 64:], low[:, :64], high[:, 64:], high[:, :64]], axis=0) * math.sqrt(POINTS)
        inv = jnp.concatenate([inv, jnp.concatenate([-inv[:, 32:], inv[:, :32]], axis=1)], axis=0)
        hi = inv.astype(BF16)
        lo = (inv - hi.astype(F32)).astype(BF16)
        left = jnp.concatenate([hi, hi, lo], axis=1)
        modes = jnp.dot(left, parts_ref[f], preferred_element_type=F32)
        out_ref[0, f] = modes[0:32]
        out_ref[1, f] = modes[32:64]
        store = pltpu.make_async_copy(out_ref.at[:, f], modes_ref.at[:, f], out_sem.at[f])
        store.start()
        stores.append(store)
    up_store.wait()
    for store in stores:
        store.wait()


def body(snapshots, weights, freq_bins):
    dma = pltpu.SemaphoreType.DMA
    hbm = pl.BlockSpec(memory_space=pltpu.HBM)
    vmem = pl.BlockSpec(memory_space=pltpu.VMEM)
    snapshots, weights, freq_bins = (pltpu.with_memory_space_constraint(a, pltpu.HBM) for a in (snapshots, weights.reshape(8, 128), freq_bins))
    parts, lower, upper = pl.pallas_call(
        gram_kernel,
        out_shape=(
            jax.ShapeDtypeStruct((FREQ, 192, LOCAL), BF16),
            jax.ShapeDtypeStruct((2, ROW, 2, 8, 128), F32),
            jax.ShapeDtypeStruct((2, 2, 8, 128), F32),
        ),
        in_specs=[hbm, hbm, hbm],
        out_specs=(vmem, vmem, vmem),
        scratch_shapes=[
            pltpu.SMEM((FREQ,), jnp.int32),
            pltpu.VMEM((8, 128), F32),
            pltpu.VMEM((CHUNKS, CHUNK, SAMPLES), BF16),
            pltpu.VMEM((ROWS, BAND), BF16),
            pltpu.VMEM((128, 128), F32),
            pltpu.VMEM((FREQ, 64, 64), F32),
            pltpu.VMEM((2, ROW, 8, 128), F32),
            pltpu.VMEM((ROW, 8, 128), F32),
            pltpu.VMEM((ROW, 8, 128), F32),
            pltpu.VMEM((ROW, 8, 128), F32),
            pltpu.VMEM((SHARES, 8, 128), F32),
            dma((2,)), dma((CHUNKS,)),
            dma((2,)), dma((2,)), dma((2,)), dma((2,)), dma((2,)), dma((2,)),
        ],
        compiler_params=pltpu.CompilerParams(
            collective_id=0, has_side_effects=True, vmem_limit_bytes=GRAM_MIB * 1024 * 1024
        ),
        cost_estimate=pl.CostEstimate(flops=2_000_000_000, bytes_accessed=11_000_000, transcendentals=0),
    )(freq_bins, weights, snapshots)
    return pl.pallas_call(
        modes_kernel,
        out_shape=(
            jax.ShapeDtypeStruct((2, FREQ, NB, LOCAL), F32),
            jax.ShapeDtypeStruct((2, 2, NB, NB), F32),
        ),
        in_specs=[vmem, vmem, vmem],
        out_specs=(hbm, hbm),
        scratch_shapes=[
            pltpu.VMEM((2, FREQ, NB, LOCAL), F32),
            pltpu.VMEM((2, 2, NB, NB), F32),
            dma((FREQ,)), dma,
        ],
        compiler_params=pltpu.CompilerParams(vmem_limit_bytes=MODES_MIB * 1024 * 1024),
        cost_estimate=pl.CostEstimate(flops=400_000_000, bytes_accessed=5_000_000, transcendentals=0),
    )(parts, lower, upper)


def solution(mesh):
    return jax.shard_map(
        body,
        mesh=mesh,
        in_specs=(P(("freq", "pts"), None), P(("freq", "pts")), P()),
        out_specs=(P(None, None, None, ("freq", "pts")), P(None, "freq", None, None)),
        check_vma=False,
    )
```

time: 36.1 us -> 31.4 us (0.87)
  local copies, waits for them, and re-layouts: 3.82 us -> 0 us
  Pallas kernels: 31.5 us -> 30.7 us
    unnamed x4 -> x0, local copies, waits for them, and re-layouts: 3.82 us -> none
    pallas_call x1 -> x2, Pallas kernels: 31.5 us -> 30.7 us  [the longest x1 28.8 us: body(): pl.pallas_call(gram_kernel, out_shape=(jax.ShapeDtypeStruct((FREQ, 192, L...]
where the time goes in v2:
time: 31.4 us; the launch traced here: 31.3 us
  Pallas kernels  30.7 us (98%)
  between operations  0.64 us (2%)
    pallas_call x1, Pallas kernels, body(): pl.pallas_call(gram_kernel, out_shape=(jax.ShapeDtypeStruct((FREQ, 192, L...  28.8 us
    pallas_call x1, Pallas kernels, body(): pl.pallas_call(modes_kernel, out_shape=(jax.ShapeDtypeStruct((2, FREQ, NB...  1.85 us

profile of v2, /device:TPU:1, one launch (start us, length us, event | category | flops | bytes accessed | tf_op | source)
XLA Modules:
  0.0 31.3 jit_solution(7558825726681251945)
XLA Ops:
  0.6 28.8 %shard_map.50 = (bf16[8,192,1024]{2,1,0:T(8,128)(2,1)S(1)}, f32[2,4,2,8,128]{4,3,2,1,0:T(8,128)S(1)}, f32[2,2,8,128]{3,2,1,0:T(8,128)S(1)}) custom-call(s32[8]{0:T(128)} %bins_ref.1, f32[8,128]{1,0:T(8,128)} %bitcast.1, bf16[1024,4224]{1,0:T(8,128)(2,1)} %snap_ref.1), custom_call_target="tpu_custom_call" | custom-call | flops 2000000000 | bytes 11000000 | tf_op jit(solution)/shard_map/pallas_call | solution.py:332
  29.5 1.8 %shard_map.51 = (f32[2,8,32,1024]{3,2,1,0:T(8,128)}, f32[2,2,32,32]{3,2,1,0:T(8,128)}) custom-call(bf16[8,192,1024]{2,1,0:T(8,128)(2,1)S(1)} %get-tuple-element.5.parts_ref, f32[2,4,2,8,128]{4,3,2,1,0:T(8,128)S(1)} %get-tuple-element.6.lower_ref, f32[2,2,8,128]{3,2,1,0:T(8,128)S(1)} %get-tuple-element.7.packed_ref), custom_call_target="tpu_custom_call" | custom-call | flops 400000000 | bytes 5000000 | tf_op jit(solution)/shard_map/pallas_call | solution.py:361

commit v3 on v2

--- a/solution.py
+++ b/solution.py
@@ -107,16 +107,15 @@
 def add_gram(parts_ref, gram_ref, chunk):
     cols = slice(chunk * CHUNK, (chunk + 1) * CHUNK)
     for f in range(FREQ):
-        hi = parts_ref[f, 0:64, cols]
-        lo = parts_ref[f, 64:128, cols]
-        s = lax.dot_general(hi, hi, NT, preferred_element_type=F32)
-        s = s + lax.dot_general(hi, lo, NT, preferred_element_type=F32)
-        s = s + lax.dot_general(lo, hi, NT, preferred_element_type=F32)
+        both = parts_ref[f, 0:128, cols]
+        s = lax.dot_general(both, both, NT, preferred_element_type=F32)
+        s = s[0:64] + s[64:128]
         gram_ref[f] = s if chunk == 0 else gram_ref[f] + s
 
 
 def packed_gram(gram_ref, f):
     s = gram_ref[f]
+    s = s[:, 0:64] + s[:, 64:128]
     gram_real = s[0:32, 0:32] + s[32:64, 32:64]
     gram_imag = s[0:32, 32:64] - s[32:64, 0:32]
     i = lax.broadcasted_iota(jnp.int32, (NB, NB), 0)
@@ -147,61 +146,66 @@
     return [whole[8 * u : 8 * u + 8] for u in range(4)], [turned[8 * u : 8 * u + 8] for u in range(4)]
 
 
-def eliminate(packed):
-    a, b = unpack_gram(packed)
-    pivots = [jnp.ones((8, 128), F32) for _ in range(4)]
+def eliminate_panel(a, b, pivots, first):
     sub = lax.broadcasted_iota(jnp.int32, (8, 128), 0)
+    v, s = first // 8, first % 8
+    last = s + WIDTH == 8
+    col_real = {u: [lanes(a[u], first + j) for j in range(WIDTH)] for u in range(v, 4)}
+    col_imag = {u: [lanes(a[u], NB + first + j) for j in range(WIDTH)] for u in range(v, 4)}
+    rows = [sublanes(a[v], s + j) for j in range(WIDTH)]
+    turned = [sublanes(b[v], s + j) for j in range(WIDTH)]
+    block_real = [[sublanes(col_real[v][l], s + i) for l in range(i + 1)] for i in range(WIDTH)]
+    block_imag = [[sublanes(col_imag[v][l], s + i) for l in range(i)] for i in range(WIDTH)]
+    over = []
+    for j in range(WIDTH):
+        pivot = block_real[j][j]
+        inverse = 1.0 / pivot
+        over.append(inverse)
+        pivots[v] = jnp.where(sub == s + j, pivot, pivots[v])
+        below = range(j + 1, WIDTH)
+        m_real = {i: block_real[i][j] * inverse for i in below}
+        m_imag = {i: block_imag[i][j] * inverse for i in below}
+        for i in below:
+            for l in range(j + 1, i + 1):
+                other_real, other_imag = block_real[l][j], block_imag[l][j]
+                block_real[i][l] = block_real[i][l] - (m_real[i] * other_real + m_imag[i] * other_imag)
+                if l < i:
+                    block_imag[i][l] = block_imag[i][l] - (m_imag[i] * other_real - m_real[i] * other_imag)
+        for i in below:
+            rows[i], turned[i] = (
+                rows[i] - (m_real[i] * rows[j] + m_imag[i] * turned[j]),
+                turned[i] - (m_real[i] * turned[j] - m_imag[i] * rows[j]),
+            )
+        for u in range(v + 1 if last else v, 4):
+            x, y = col_real[u][j], col_imag[u][j]
+            for l in below:
+                col_real[u][l] = col_real[u][l] - (x * m_real[l] + y * m_imag[l])
+                col_imag[u][l] = col_imag[u][l] - (y * m_real[l] - x * m_imag[l])
+    for u in range(v, 4):
+        new_a, new_b = a[u], b[u]
+        if u > v or not last:
+            for j in range(WIDTH):
+                x, y = col_real[u][j], col_imag[u][j]
+                row, row_turned = rows[j] * over[j], turned[j] * over[j]
+                new_a = new_a - (x * row + y * row_turned)
+                new_b = new_b - (x * row_turned - y * row)
+            if u == v and s > 0:
+                new_a = jnp.where(sub < s, a[u], new_a)
+                new_b = jnp.where(sub < s, b[u], new_b)
+        if u == v:
+            for j in range(WIDTH):
+                new_a = jnp.where(sub == s + j, rows[j], new_a)
+                new_b = jnp.where(sub == s + j, turned[j], new_b)
+        a[u], b[u] = new_a, new_b
+
+
+def eliminate(packs):
+    states = [unpack_gram(packed) for packed in packs]
+    pivots = [[jnp.ones((8, 128), F32) for _ in range(4)] for _ in packs]
     for first in range(0, NB, WIDTH):
-        v, s = first // 8, first % 8
-        last = s + WIDTH == 8
-        col_real = {u: [lanes(a[u], first + j) for j in range(WIDTH)] for u in range(v, 4)}
-        col_imag = {u: [lanes(a[u], NB + first + j) for j in range(WIDTH)] for u in range(v, 4)}
-        rows = [sublanes(a[v], s + j) for j in range(WIDTH)]
-        turned = [sublanes(b[v], s + j) for j in range(WIDTH)]
-        block_real = [[sublanes(col_real[v][l], s + i) for l in range(i + 1)] for i in range(WIDTH)]
-        block_imag = [[sublanes(col_imag[v][l], s + i) for l in range(i)] for i in range(WIDTH)]
-        over = []
-        for j in range(WIDTH):
-            pivot = block_real[j][j]
-            inverse = 1.0 / pivot
-            over.append(inverse)
-            pivots[v] = jnp.where(sub == s + j, pivot, pivots[v])
-            below = range(j + 1, WIDTH)
-            m_real = {i: block_real[i][j] * inverse for i in below}
-            m_imag = {i: block_imag[i][j] * inverse for i in below}
-            for i in below:
-                for l in range(j + 1, i + 1):
-                    other_real, other_imag = block_real[l][j], block_imag[l][j]
-                    block_real[i][l] = block_real[i][l] - (m_real[i] * other_real + m_imag[i] * other_imag)
-                    if l < i:
-                        block_imag[i][l] = block_imag[i][l] - (m_imag[i] * other_real - m_real[i] * other_imag)
-            for i in below:
-                rows[i], turned[i] = (
-                    rows[i] - (m_real[i] * rows[j] + m_imag[i] * turned[j]),
-                    turned[i] - (m_real[i] * turned[j] - m_imag[i] * rows[j]),
-                )
-            for u in range(v + 1 if last else v, 4):
-                x, y = col_real[u][j], col_imag[u][j]
-                for l in below:
-                    col_real[u][l] = col_real[u][l] - (x * m_real[l] + y * m_imag[l])
-                    col_imag[u][l] = col_imag[u][l] - (y * m_real[l] - x * m_imag[l])
-        for u in range(v, 4):
-            new_a, new_b = a[u], b[u]
-            if u > v or not last:
-                for j in range(WIDTH):
-                    x, y = col_real[u][j], col_imag[u][j]
-                    row, row_turned = rows[j] * over[j], turned[j] * over[j]
-                    new_a = new_a - (x * row + y * row_turned)
-                    new_b = new_b - (x * row_turned - y * row)
-                if u == v and s > 0:
-                    new_a = jnp.where(sub < s, a[u], new_a)
-                    new_b = jnp.where(sub < s, b[u], new_b)
-            if u == v:
-                for j in range(WIDTH):
-                    new_a = jnp.where(sub == s + j, rows[j], new_a)
-                    new_b = jnp.where(sub == s + j, turned[j], new_b)
-            a[u], b[u] = new_a, new_b
-    return [a[u] * (1.0 / jnp.sqrt(pivots[u])) for u in range(4)]
+        for (a, b), pivot in zip(states, pivots):
+            eliminate_panel(a, b, pivot, first)
+    return [[a[u] * (1.0 / jnp.sqrt(pivot[u])) for u in range(4)] for (a, b), pivot in zip(states, pivots)]
 
 
 def wait_bytes(ref, sem):
@@ -210,8 +214,8 @@
 
 def gram_kernel(
     bins_ref, weights_ref, snap_ref, parts_ref, lower_ref, upper_ref,
-    bins_here, weights_here, x_ref, band_ref, sums_ref, gram_ref, pack_ref, got_s, half_ref, got_x, got_p,
-    small_sem, in_sem, s_sems, x_sems, p_sems, l_sems, c_sems, r_sems,
+    bins_here, weights_here, x_ref, band_ref, sums_ref, gram_ref, pack_ref, got_s, got_x, got_p, all_upper,
+    small_sem, in_sem, s_sems, x_sems, p_sems, c_sems, r_sems,
 ):
     x, share, core = place()
     sibling = (x, share * 2 + 1 - core)
@@ -245,51 +249,48 @@
     for chunk in range(CHUNKS):
         loads[chunk].wait()
         transform_chunk(chunk, weights_here, x_ref, band_ref, sums_ref, parts_ref)
-        add_gram(parts_ref, gram_ref, chunk)
+        if chunk > 0:
+            add_gram(parts_ref, gram_ref, chunk - 1)
+    add_gram(parts_ref, gram_ref, CHUNKS - 1)
     for f in range(FREQ):
         pack_ref[f % 2, f // 2] = packed_gram(gram_ref, f)
     pl.semaphore_wait(barrier, 1 + ROW - 1 + SHARES - 1)
 
     send(pack_ref.at[1 - core], got_s, s_sems, sibling)
     wait_bytes(got_s, s_sems.at[1])
-    half_ref[...] = pack_ref[core] + got_s[...]
+    got_x[x] = pack_ref[core] + got_s[...]
 
     for step in ROW_STEPS:
-        other, device = row_peer(x, share, core, step)
-        send(half_ref.at[other], got_x.at[x], x_sems, device)
-    got_x[x] = half_ref[x]
+        send(got_x.at[x], got_x.at[x], x_sems, row_peer(x, share, core, step)[1])
     wait_bytes(got_x.at[0 : ROW - 1], x_sems.at[1])
     got_p[share] = (got_x[0] + got_x[1]) + (got_x[2] + got_x[3])
 
     for step in PLANE_STEPS:
-        other, device = plane_peer(x, share, core, step)
-        send(got_p.at[share], got_p.at[share], p_sems, device)
+        send(got_p.at[share], got_p.at[share], p_sems, plane_peer(x, share, core, step)[1])
     wait_bytes(got_p.at[0 : SHARES - 1], p_sems.at[1])
-    terms = [got_p[n] for n in range(SHARES)]
-    while len(terms) > 1:
-        terms = [terms[n] + terms[n + 1] for n in range(0, len(terms), 2)]
-
-    rows = eliminate(terms[0])
+    packs = []
+    for n in range(FREQ // 2):
+        terms = [got_p[m, n] for m in range(SHARES)]
+        while len(terms) > 1:
+            terms = [terms[m] + terms[m + 1] for m in range(0, len(terms), 2)]
+        packs.append(terms[0])
+
     lane = lax.broadcasted_iota(jnp.int32, (8, 128), 1)
-    for h in range(2):
-        even, odd = rows[2 * h], rows[2 * h + 1]
-        odd_far = pltpu.roll(odd, 64, 1)
-        lower_ref[core, x, h] = jnp.where(lane < 64, odd_far, even)
-        upper_ref[core, h] = jnp.where(lane < 64, even, odd_far)
-    mine = lower_ref.at[core, x]
-    for step in ROW_STEPS:
-        other, device = row_peer(x, share, core, step)
-        send(mine, mine, l_sems, device)
+    for n, rows in enumerate(eliminate(packs)):
+        for h in range(2):
+            even, odd = rows[2 * h], rows[2 * h + 1]
+            odd_far = pltpu.roll(odd, 64, 1)
+            lower_ref[core, n, h] = jnp.where(lane < 64, odd_far, even)
+            all_upper[n, h] = jnp.where(lane < 64, even, odd_far)
+    send(lower_ref.at[core], lower_ref.at[core], c_sems, sibling)
+    upper_ref[core] = all_upper[x]
     send(upper_ref.at[core], upper_ref.at[core], r_sems, sibling)
-    wait_bytes(lower_ref.at[0, 0 : ROW - 1], l_sems.at[1])
-    send(lower_ref.at[core], lower_ref.at[core], c_sems, sibling)
     wait_bytes(lower_ref.at[0], c_sems.at[1])
     wait_bytes(upper_ref.at[0], r_sems.at[1])
 
     wait_bytes(got_s, s_sems.at[0])
     wait_bytes(got_x.at[0 : ROW - 1], x_sems.at[0])
     wait_bytes(got_p.at[0 : SHARES - 1], p_sems.at[0])
-    wait_bytes(lower_ref.at[0, 0 : ROW - 1], l_sems.at[0])
     wait_bytes(lower_ref.at[0], c_sems.at[0])
     wait_bytes(upper_ref.at[0], r_sems.at[0])
 
@@ -344,14 +345,14 @@
             pltpu.VMEM((CHUNKS, CHUNK, SAMPLES), BF16),
             pltpu.VMEM((ROWS, BAND), BF16),
             pltpu.VMEM((128, 128), F32),
-            pltpu.VMEM((FREQ, 64, 64), F32),
+            pltpu.VMEM((FREQ, 64, 128), F32),
             pltpu.VMEM((2, ROW, 8, 128), F32),
             pltpu.VMEM((ROW, 8, 128), F32),
-            pltpu.VMEM((ROW, 8, 128), F32),
-            pltpu.VMEM((ROW, 8, 128), F32),
-            pltpu.VMEM((SHARES, 8, 128), F32),
+            pltpu.VMEM((ROW, ROW, 8, 128), F32),
+            pltpu.VMEM((SHARES, ROW, 8, 128), F32),
+            pltpu.VMEM((ROW, 2, 8, 128), F32),
             dma((2,)), dma((CHUNKS,)),
-            dma((2,)), dma((2,)), dma((2,)), dma((2,)), dma((2,)), dma((2,)),
+            dma((2,)), dma((2,)), dma((2,)), dma((2,)), dma((2,)),
         ],
         compiler_params=pltpu.CompilerParams(
             collective_id=0, has_side_effects=True, vmem_limit_bytes=GRAM_MIB * 1024 * 1024

time: 31.4 us -> 30.4 us (0.968)
  Pallas kernels: 30.7 us -> 29.6 us
    pallas_call x1, Pallas kernels: 28.8 us -> 27.8 us  [body(): pl.pallas_call(gram_kernel, out_shape=(jax.ShapeDtypeStruct((FREQ, 192, L...]
where the time goes in v3:
time: 30.4 us; the launch traced here: 30.3 us
  Pallas kernels  29.6 us (97%)
  between operations  0.64 us (2%)
    pallas_call x1, Pallas kernels, body(): pl.pallas_call(gram_kernel, out_shape=(jax.ShapeDtypeStruct((FREQ, 192, L...  27.8 us
    pallas_call x1, Pallas kernels, body(): pl.pallas_call(modes_kernel, out_shape=(jax.ShapeDtypeStruct((2, FREQ, NB...  1.84 us

profile of v3, /device:TPU:1, one launch (start us, length us, event | category | flops | bytes accessed | tf_op | source)
XLA Modules:
  0.0 30.3 jit_solution(9823922446455997681)
XLA Ops:
  0.6 27.8 %shard_map.50 = (bf16[8,192,1024]{2,1,0:T(8,128)(2,1)S(1)}, f32[2,4,2,8,128]{4,3,2,1,0:T(8,128)S(1)}, f32[2,2,8,128]{3,2,1,0:T(8,128)S(1)}) custom-call(s32[8]{0:T(128)} %bins_ref.1, f32[8,128]{1,0:T(8,128)} %bitcast.1, bf16[1024,4224]{1,0:T(8,128)(2,1)} %snap_ref.1), custom_call_target="tpu_custom_call" | custom-call | flops 2000000000 | bytes 11000000 | tf_op jit(solution)/shard_map/pallas_call | solution.py:333
  28.4 1.8 %shard_map.51 = (f32[2,8,32,1024]{3,2,1,0:T(8,128)}, f32[2,2,32,32]{3,2,1,0:T(8,128)}) custom-call(bf16[8,192,1024]{2,1,0:T(8,128)(2,1)S(1)} %get-tuple-element.5.parts_ref, f32[2,4,2,8,128]{4,3,2,1,0:T(8,128)S(1)} %get-tuple-element.6.lower_ref, f32[2,2,8,128]{3,2,1,0:T(8,128)S(1)} %get-tuple-element.7.packed_ref), custom_call_target="tpu_custom_call" | custom-call | flops 400000000 | bytes 5000000 | tf_op jit(solution)/shard_map/pallas_call | solution.py:362

commit v4 on v3

--- a/solution.py
+++ b/solution.py
@@ -76,17 +76,18 @@
     sums_ref[...] = jnp.dot(band_ref[0:128, :], ones, preferred_element_type=F32)
 
 
-def transform_chunk(chunk, weights_ref, x_ref, band_ref, sums_ref, parts_ref):
+def multiply_chunk(chunk, x_ref, band_ref, held_ref):
     band = band_ref[...]
-    groups = []
-    total = jnp.zeros((1, CHUNK), F32)
     for g in range(GROUPS):
         x = x_ref[chunk, :, g * 8 * HALF : g * 8 * HALF + BAND]
-        d = lax.dot_general(band, x, NT, preferred_element_type=F32)
-        groups.append(d)
-        total = total + d[128:129]
-        if g == GROUPS - 1:
-            total = total + d[129:130]
+        held_ref[chunk % 2, g] = lax.dot_general(band, x, NT, preferred_element_type=F32)
+
+
+def finish_chunk(chunk, weights_ref, held_ref, sums_ref, parts_ref):
+    held = held_ref.at[chunk % 2]
+    total = held[GROUPS - 1, 129:130, :]
+    for g in range(GROUPS):
+        total = total + held[g, 128:129, :]
     mean = total * (1.0 / SAMPLES)
     w = jnp.concatenate([weights_ref[2 * chunk : 2 * chunk + 1], weights_ref[2 * chunk + 1 : 2 * chunk + 2]], axis=1)
     scale = jnp.sqrt(w * (1.0 / POINTS)) * (1.0 / math.sqrt(NB * 0.375 * NFFT))
@@ -96,7 +97,7 @@
             c = part * FREQ + f
             sums = sums_ref[c * 8 : c * 8 + 8, :]
             away = jnp.concatenate([sums, sums], axis=1) * mean
-            y = jnp.concatenate([(d[c * 8 : c * 8 + 8] - away) * scale for d in groups], axis=0)
+            y = jnp.concatenate([(held[g, c * 8 : c * 8 + 8, :] - away) * scale for g in range(GROUPS)], axis=0)
             hi = y.astype(BF16)
             lo = (y - hi.astype(F32)).astype(BF16)
             parts_ref[f, part * NB : (part + 1) * NB, cols] = hi
@@ -214,43 +215,52 @@
 
 def gram_kernel(
     bins_ref, weights_ref, snap_ref, parts_ref, lower_ref, upper_ref,
-    bins_here, weights_here, x_ref, band_ref, sums_ref, gram_ref, pack_ref, got_s, got_x, got_p, all_upper,
+    bins_here, weights_here, x_ref, band_ref, sums_ref, held_ref, gram_ref, pack_ref, got_s, got_x, got_p, all_upper,
     small_sem, in_sem, s_sems, x_sems, p_sems, c_sems, r_sems,
 ):
     x, share, core = place()
     sibling = (x, share * 2 + 1 - core)
+    def send(src, dst, sems, device):
+        pltpu.make_async_remote_copy(
+            src_ref=src, dst_ref=dst, send_sem=sems.at[0], recv_sem=sems.at[1], device_id=device, device_id_type=MESH
+        ).start()
+
+    barrier = pltpu.get_barrier_semaphore()
+
+    def greet(device):
+        pl.semaphore_signal(barrier, inc=1, device_id=device, device_id_type=MESH)
+
     smalls = [
         pltpu.make_async_copy(bins_ref, bins_here, small_sem.at[0]),
         pltpu.make_async_copy(weights_ref, weights_here, small_sem.at[1]),
     ]
     for small in smalls:
         small.start()
-    loads = []
-    for chunk in range(CHUNKS):
-        load = pltpu.make_async_copy(snap_ref.at[chunk * CHUNK : (chunk + 1) * CHUNK, :], x_ref.at[chunk], in_sem.at[chunk])
+    loads = [
+        pltpu.make_async_copy(snap_ref.at[chunk * CHUNK : (chunk + 1) * CHUNK, :], x_ref.at[chunk], in_sem.at[chunk])
+        for chunk in range(CHUNKS)
+    ]
+    loads[0].start()
+    for step in PLANE_STEPS[:8]:
+        greet(plane_peer(x, share, core, step)[1])
+    loads[1].start()
+    for step in PLANE_STEPS[8:]:
+        greet(plane_peer(x, share, core, step)[1])
+    for load in loads[2:]:
         load.start()
-        loads.append(load)
-
-    def send(src, dst, sems, device):
-        pltpu.make_async_remote_copy(
-            src_ref=src, dst_ref=dst, send_sem=sems.at[0], recv_sem=sems.at[1], device_id=device, device_id_type=MESH
-        ).start()
-
-    barrier = pltpu.get_barrier_semaphore()
-    pl.semaphore_signal(barrier, inc=1, device_id=sibling, device_id_type=MESH)
-    for step in ROW_STEPS:
-        pl.semaphore_signal(barrier, inc=1, device_id=row_peer(x, share, core, step)[1], device_id_type=MESH)
-    for step in PLANE_STEPS:
-        pl.semaphore_signal(barrier, inc=1, device_id=plane_peer(x, share, core, step)[1], device_id_type=MESH)
-
     for small in smalls:
         small.wait()
     build_band(bins_here, band_ref, sums_ref)
+    for step in ROW_STEPS:
+        greet(row_peer(x, share, core, step)[1])
+    greet(sibling)
     for chunk in range(CHUNKS):
         loads[chunk].wait()
-        transform_chunk(chunk, weights_here, x_ref, band_ref, sums_ref, parts_ref)
+        multiply_chunk(chunk, x_ref, band_ref, held_ref)
         if chunk > 0:
+            finish_chunk(chunk - 1, weights_here, held_ref, sums_ref, parts_ref)
             add_gram(parts_ref, gram_ref, chunk - 1)
+    finish_chunk(CHUNKS - 1, weights_here, held_ref, sums_ref, parts_ref)
     add_gram(parts_ref, gram_ref, CHUNKS - 1)
     for f in range(FREQ):
         pack_ref[f % 2, f // 2] = packed_gram(gram_ref, f)
@@ -345,6 +355,7 @@
             pltpu.VMEM((CHUNKS, CHUNK, SAMPLES), BF16),
             pltpu.VMEM((ROWS, BAND), BF16),
             pltpu.VMEM((128, 128), F32),
+            pltpu.VMEM((2, GROUPS, ROWS, CHUNK), F32),
             pltpu.VMEM((FREQ, 64, 128), F32),
             pltpu.VMEM((2, ROW, 8, 128), F32),
             pltpu.VMEM((ROW, 8, 128), F32),

time: 30.4 us -> 28.7 us (0.944)
  Pallas kernels: 29.6 us -> 28 us
    pallas_call x1, Pallas kernels: 27.8 us -> 26.1 us  [body(): pl.pallas_call(gram_kernel, out_shape=(jax.ShapeDtypeStruct((FREQ, 192, L...]
where the time goes in v4:
time: 28.7 us; the launch traced here: 28.6 us
  Pallas kernels  28 us (98%)
  between operations  0.64 us (2%)
    pallas_call x1, Pallas kernels, body(): pl.pallas_call(gram_kernel, out_shape=(jax.ShapeDtypeStruct((FREQ, 192, L...  26.1 us
    pallas_call x1, Pallas kernels, body(): pl.pallas_call(modes_kernel, out_shape=(jax.ShapeDtypeStruct((2, FREQ, NB...  1.85 us

profile of v4, /device:TPU:1, one launch (start us, length us, event | category | flops | bytes accessed | tf_op | source)
XLA Modules:
  0.0 28.6 jit_solution(5210832131947670942)
XLA Ops:
  0.6 26.1 %shard_map.50 = (bf16[8,192,1024]{2,1,0:T(8,128)(2,1)S(1)}, f32[2,4,2,8,128]{4,3,2,1,0:T(8,128)S(1)}, f32[2,2,8,128]{3,2,1,0:T(8,128)S(1)}) custom-call(s32[8]{0:T(128)} %bins_ref.1, f32[8,128]{1,0:T(8,128)} %bitcast.1, bf16[1024,4224]{1,0:T(8,128)(2,1)} %snap_ref.1), custom_call_target="tpu_custom_call" | custom-call | flops 2000000000 | bytes 11000000 | tf_op jit(solution)/shard_map/pallas_call | solution.py:343
  26.8 1.8 %shard_map.51 = (f32[2,8,32,1024]{3,2,1,0:T(8,128)}, f32[2,2,32,32]{3,2,1,0:T(8,128)}) custom-call(bf16[8,192,1024]{2,1,0:T(8,128)(2,1)S(1)} %get-tuple-element.5.parts_ref, f32[2,4,2,8,128]{4,3,2,1,0:T(8,128)S(1)} %get-tuple-element.6.lower_ref, f32[2,2,8,128]{3,2,1,0:T(8,128)S(1)} %get-tuple-element.7.packed_ref), custom_call_target="tpu_custom_call" | custom-call | flops 400000000 | bytes 5000000 | tf_op jit(solution)/shard_map/pallas_call | solution.py:373

commit v5 on v4

--- a/solution.py
+++ b/solution.py
@@ -83,7 +83,7 @@
         held_ref[chunk % 2, g] = lax.dot_general(band, x, NT, preferred_element_type=F32)
 
 
-def finish_chunk(chunk, weights_ref, held_ref, sums_ref, parts_ref):
+def finish_chunk(chunk, freqs, weights_ref, held_ref, sums_ref, parts_ref):
     held = held_ref.at[chunk % 2]
     total = held[GROUPS - 1, 129:130, :]
     for g in range(GROUPS):
@@ -92,12 +92,12 @@
     w = jnp.concatenate([weights_ref[2 * chunk : 2 * chunk + 1], weights_ref[2 * chunk + 1 : 2 * chunk + 2]], axis=1)
     scale = jnp.sqrt(w * (1.0 / POINTS)) * (1.0 / math.sqrt(NB * 0.375 * NFFT))
     cols = slice(chunk * CHUNK, (chunk + 1) * CHUNK)
-    for f in range(FREQ):
+    for f in freqs:
         for part in range(2):
-            c = part * FREQ + f
-            sums = sums_ref[c * 8 : c * 8 + 8, :]
+            rows = pl.ds(part * FREQ * 8 + f * 8 if isinstance(f, int) else pl.multiple_of(part * FREQ * 8 + f * 8, 8), 8)
+            sums = sums_ref[rows, :]
             away = jnp.concatenate([sums, sums], axis=1) * mean
-            y = jnp.concatenate([(held[g, c * 8 : c * 8 + 8, :] - away) * scale for g in range(GROUPS)], axis=0)
+            y = jnp.concatenate([(held[g, rows, :] - away) * scale for g in range(GROUPS)], axis=0)
             hi = y.astype(BF16)
             lo = (y - hi.astype(F32)).astype(BF16)
             parts_ref[f, part * NB : (part + 1) * NB, cols] = hi
@@ -105,9 +105,9 @@
             parts_ref[f, 128 + part * NB : 128 + (part + 1) * NB, cols] = hi
 
 
-def add_gram(parts_ref, gram_ref, chunk):
+def add_gram(chunk, freqs, parts_ref, gram_ref):
     cols = slice(chunk * CHUNK, (chunk + 1) * CHUNK)
-    for f in range(FREQ):
+    for f in freqs:
         both = parts_ref[f, 0:128, cols]
         s = lax.dot_general(both, both, NT, preferred_element_type=F32)
         s = s[0:64] + s[64:128]
@@ -246,29 +246,32 @@
     loads[1].start()
     for step in PLANE_STEPS[8:]:
         greet(plane_peer(x, share, core, step)[1])
-    for load in loads[2:]:
-        load.start()
     for small in smalls:
         small.wait()
     build_band(bins_here, band_ref, sums_ref)
     for step in ROW_STEPS:
         greet(row_peer(x, share, core, step)[1])
     greet(sibling)
+    loads[2].start()
     for chunk in range(CHUNKS):
         loads[chunk].wait()
+        if chunk == 0:
+            loads[3].start()
         multiply_chunk(chunk, x_ref, band_ref, held_ref)
         if chunk > 0:
-            finish_chunk(chunk - 1, weights_here, held_ref, sums_ref, parts_ref)
-            add_gram(parts_ref, gram_ref, chunk - 1)
-    finish_chunk(CHUNKS - 1, weights_here, held_ref, sums_ref, parts_ref)
-    add_gram(parts_ref, gram_ref, CHUNKS - 1)
-    for f in range(FREQ):
-        pack_ref[f % 2, f // 2] = packed_gram(gram_ref, f)
-    pl.semaphore_wait(barrier, 1 + ROW - 1 + SHARES - 1)
-
-    send(pack_ref.at[1 - core], got_s, s_sems, sibling)
+            finish_chunk(chunk - 1, range(FREQ), weights_here, held_ref, sums_ref, parts_ref)
+            add_gram(chunk - 1, range(FREQ), parts_ref, gram_ref)
+    for side in range(2):
+        freqs = [2 * n + (1 - core if side == 0 else core) for n in range(FREQ // 2)]
+        finish_chunk(CHUNKS - 1, freqs, weights_here, held_ref, sums_ref, parts_ref)
+        add_gram(CHUNKS - 1, freqs, parts_ref, gram_ref)
+        for n in range(FREQ // 2):
+            pack_ref[side, n] = packed_gram(gram_ref, freqs[n])
+        if side == 0:
+            pl.semaphore_wait(barrier, 1 + ROW - 1 + SHARES - 1)
+            send(pack_ref.at[0], got_s, s_sems, sibling)
     wait_bytes(got_s, s_sems.at[1])
-    got_x[x] = pack_ref[core] + got_s[...]
+    got_x[x] = pack_ref[1] + got_s[...]
 
     for step in ROW_STEPS:
         send(got_x.at[x], got_x.at[x], x_sems, row_peer(x, share, core, step)[1])

time: 28.7 us -> 28.5 us (level)
  no operation moved by 1% of the time
where the time goes in v5:
time: 28.5 us; the launch traced here: 28.4 us
  Pallas kernels  27.8 us (98%)
  between operations  0.64 us (2%)
    pallas_call x1, Pallas kernels, body(): pl.pallas_call(gram_kernel, out_shape=(jax.ShapeDtypeStruct((FREQ, 192, L...  25.9 us
    pallas_call x1, Pallas kernels, body(): pl.pallas_call(modes_kernel, out_shape=(jax.ShapeDtypeStruct((2, FREQ, NB...  1.85 us

profile of v5, /device:TPU:1, one launch (start us, length us, event | category | flops | bytes accessed | tf_op | source)
XLA Modules:
  0.0 28.4 jit_solution(14891000850350831086)
XLA Ops:
  0.6 25.9 %shard_map.50 = (bf16[8,192,1024]{2,1,0:T(8,128)(2,1)S(1)}, f32[2,4,2,8,128]{4,3,2,1,0:T(8,128)S(1)}, f32[2,2,8,128]{3,2,1,0:T(8,128)S(1)}) custom-call(s32[8]{0:T(128)} %bins_ref.1, f32[8,128]{1,0:T(8,128)} %bitcast.1, bf16[1024,4224]{1,0:T(8,128)(2,1)} %snap_ref.1), custom_call_target="tpu_custom_call" | custom-call | flops 2000000000 | bytes 11000000 | tf_op jit(solution)/shard_map/pallas_call | solution.py:346
  26.6 1.8 %shard_map.51 = (f32[2,8,32,1024]{3,2,1,0:T(8,128)}, f32[2,2,32,32]{3,2,1,0:T(8,128)}) custom-call(bf16[8,192,1024]{2,1,0:T(8,128)(2,1)S(1)} %get-tuple-element.5.parts_ref, f32[2,4,2,8,128]{4,3,2,1,0:T(8,128)S(1)} %get-tuple-element.6.lower_ref, f32[2,2,8,128]{3,2,1,0:T(8,128)S(1)} %get-tuple-element.7.packed_ref), custom_call_target="tpu_custom_call" | custom-call | flops 400000000 | bytes 5000000 | tf_op jit(solution)/shard_map/pallas_call | solution.py:376
